TPU v7x, 32 devices: a whole 2x2x4 slice. The times are simulated.
32 devices in a mesh: tm: 8 (over z, x), rows: 4 (over y, core).
Axes of the slice: x: 2, y: 2, z: 4, core: 2. Of those that a mesh axis runs over, the one named last changes fastest.
Arguments:
- x_start: float32 [1, 16, 64, 128], P(None, None, 'rows'), may hold values from -6 to 6
- noise: float32 [8, 1, 16, 64, 128], P('tm', None, None, 'rows'), may hold values from -6 to 6
- fresh: float32 [5, 1, 16, 64, 128], P(None, None, None, 'rows'), may hold values from -6 to 6
- sched: int32 [14], replicated, may hold values from 960 to 999, as said below
- conv_in: bfloat16 [3, 3, 192, 16], replicated, may hold values from -0.5 to 0.5
- conv_mid: bfloat16 [3, 3, 192, 192], replicated, may hold values from -0.15625 to 0.15625
- conv_out: bfloat16 [3, 3, 16, 192], replicated, may hold values from -0.15625 to 0.15625
- time_weight: bfloat16 [192, 192], replicated, may hold values from -0.4375 to 0.4375
Outputs:
- trajectory: float32 [2, 8, 1, 16, 64, 128], P(None, 'tm', None, None, 'rows')
Inputs may be any that keep to these rules, and one draw needn't show every extreme that they name: sched[0] = 999 and each entry is 1 to 3 below the one before it.
All inputs are finite; a program needn't handle non-finite values.
Results may differ from a plain program's by a relative error of at most 0.00055.
Values may be sent and summed in bfloat16 or wider, within the bound.
A program may use at most 64 MiB of HBM per device.

v0:
```python
import functools

import jax
import jax.numpy as jnp
import numpy as np
from jax import lax
from jax.experimental import pallas as pl
from jax.experimental.pallas import tpu as pltpu
from jax.sharding import PartitionSpec as P

STEPS = 1000
RETIRE = 5
ROUNDS = 2
RIM = 3

log_base = 9.210340371976184
MESH = pl.DeviceIdType.MESH
f32, bf16 = jnp.float32, jnp.bfloat16


def plan_table(total_steps):
    positions = np.arange(total_steps).astype(np.float64)
    betas = 0.0001 + (0.02 - 0.0001) * positions / (total_steps - 1)
    return jnp.asarray(np.cumsum(np.log(1.0 - betas)).astype(np.float32))


def lookup(table, position):
    hit = jnp.arange(table.shape[0])[None] == position[:, None]
    return jnp.sum(jnp.where(hit, table[None], 0.0), axis=1)


def coefficients(log_now, log_next):
    retained = jnp.exp(log_now - log_next)
    bar_now = jnp.exp(log_now)
    bar_next = jnp.exp(log_next)
    keep = 1.0 / jnp.sqrt(retained) - 1.0
    predict = -(1.0 - retained) / (jnp.sqrt(1.0 - bar_now) * jnp.sqrt(retained))
    spread = jnp.sqrt((1.0 - bar_next) / (1.0 - bar_now) * (1.0 - retained))
    return jnp.stack([keep, predict, spread], axis=1)


def time_features(now_value, width):
    half = width // 2
    freqs = jnp.exp(-log_base * jnp.arange(half).astype(f32) / half)
    angles = now_value[..., None] * freqs
    return jnp.concatenate([jnp.sin(angles), jnp.cos(angles)], axis=-1)


def silu(v):
    half = 0.5 * v
    return half + half * jnp.tanh(half)


def moved_right(v):
    lane = lax.broadcasted_iota(jnp.int32, v.shape, v.ndim - 1)
    return jnp.where(lane == 0, 0.0, pltpu.roll(v, 1, v.ndim - 1))


def moved_left(v):
    size = v.shape[-1]
    lane = lax.broadcasted_iota(jnp.int32, v.shape, v.ndim - 1)
    return jnp.where(lane == size - 1, 0.0, pltpu.roll(v, size - 1, v.ndim - 1))


def kernel(
    n, strips, hops,
    coef, x, z0, entrant, emb, w_in, w_mid, w_out, out,
    st, first, parts, state, exc, inc, nexc, ninc, base, base_src,
    sent_state, rim, arrived, z_arrived,
    snd, rcv, nsnd, nrcv,
    rim_ss, rim_rs, far_ss, mv_ss, mv_rs, z_ss, z_rs,
    scan_ss, scan_rs, nscan_ss, nscan_rs, base_ss, base_rs,
):
    me, strip = lax.axis_index("tm"), lax.axis_index("rows")
    rows, chans, cols = x.shape
    hidden = w_mid.shape[0]
    stay = n - RETIRE
    has_up, has_down = strip > 0, strip < strips - 1

    def remote(src, dst, ss, rs, slot, to_strip):
        return pltpu.make_async_remote_copy(
            src_ref=src, dst_ref=dst, send_sem=ss, recv_sem=rs,
            device_id=(jnp.clip(slot, 0, n - 1), jnp.clip(to_strip, 0, strips - 1)),
            device_id_type=MESH,
        )

    def rim_copy(k, side, slot, far):
        lo = rows - RIM if side == 0 else 0
        to = strip + 1 if side == 0 else strip - 1
        ss = far_ss.at[side] if far else rim_ss.at[k, side]
        return remote(sent_state.at[k, pl.ds(lo, RIM)], rim.at[k, side], ss, rim_rs.at[k, side], slot, to)

    def send_rim(k, slot, far, gate, start):
        for side, there in ((0, has_down), (1, has_up)):
            @pl.when(jnp.logical_and(gate, there))
            def _():
                copy = rim_copy(k, side, slot, far)
                copy.start() if start else copy.wait_send()

    def move_copy():
        return remote(sent_state.at[2], arrived, mv_ss, mv_rs, me - RETIRE, strip)

    def z_copy():
        return remote(z0, z_arrived, z_ss, z_rs, me - RETIRE, strip)

    def base_copy(slot):
        return remote(base_src, base, base_ss.at[slot], base_rs, slot, strip)

    def scan_copy(k, s):
        return remote(snd.at[k, s], rcv.at[k, s], scan_ss.at[k, s], scan_rs.at[k, s], me + 2**s, strip)

    def nscan_copy(k, s):
        return remote(nsnd.at[k, s], nrcv.at[k, s], nscan_ss.at[k, s], nscan_rs.at[k, s], me + 2**s, strip)

    def spread_rows(v):
        v = v.astype(f32)
        return jnp.concatenate([moved_right(v), v, moved_left(v)], axis=-2).astype(bf16)

    def expand(source, at, count):
        for i in range(count):
            st[at + i] = spread_rows(source[i])

    def noise_send(k, s):
        @pl.when(me + 2**s < n)
        def _():
            nsnd[k, s] = ninc[k]
            nscan_copy(k, s).start()

    def noise_take(k, s):
        @pl.when(me >= 2**s)
        def _():
            nscan_copy(k, s).wait_recv()
            nexc[k] += nrcv[k, s]
            ninc[k] += nrcv[k, s]

    def noise_advance(k, s):
        if s < hops:
            noise_take(k, s)
        if s + 1 < hops:
            noise_send(k, s + 1)

    def noise_finish(k, s):
        for t in range(s, hops):
            noise_advance(k, t)

    def network(r):
        embedding = emb.at[r]

        def in_step(i, _):
            f = 2 * i
            both = jnp.concatenate(
                [st[pl.ds(f + t, 3)].reshape(9 * chans, cols) for t in range(2)], axis=1
            )
            h = jnp.dot(w_in[...], both, preferred_element_type=f32)
            for t in range(2):
                v = silu(h[:, t * cols : (t + 1) * cols] + embedding[...])
                first[f + t] = spread_rows(v)
            return 0

        lax.fori_loop(0, (rows + 4) // 2, in_step, 0, unroll=2)

        @pl.when(jnp.logical_not(has_up))
        def _():
            first[pl.ds(0, 2)] = jnp.zeros((2,) + first.shape[1:], bf16)

        @pl.when(jnp.logical_not(has_down))
        def _():
            first[pl.ds(rows + 2, 2)] = jnp.zeros((2,) + first.shape[1:], bf16)

        def mid_step(i, _):
            f = 2 * i
            both = jnp.concatenate(
                [first[pl.ds(f + t, 3)].reshape(9 * hidden, cols) for t in range(2)], axis=1
            )
            g = silu(jnp.dot(w_mid[...], both, preferred_element_type=f32)).astype(bf16)
            p = jnp.dot(w_out[...], g, preferred_element_type=f32)
            for t in range(2):
                parts[f + t] = p[:, t * cols : (t + 1) * cols]
            return 0

        lax.fori_loop(0, (rows + 2) // 2, mid_step, 0, unroll=3)

        @pl.when(jnp.logical_not(has_up))
        def _():
            parts[0] = jnp.zeros(parts.shape[1:], f32)

        @pl.when(jnp.logical_not(has_down))
        def _():
            parts[rows + 1] = jnp.zeros(parts.shape[1:], f32)

    def finish(k, r, noise):
        keep, predict, spread = coef[r, 0], coef[r, 1], coef[r, 2]

        def row(y, _):
            sums = [
                sum(parts[y + a, pl.ds((3 * a + b) * chans, chans)] for a in range(3))
                for b in range(3)
            ]
            predicted = moved_right(sums[0]) + sums[1] + moved_left(sums[2])
            c = keep * state[y] + predict * predicted
            if noise is not None:
                c = c + spread * noise[y]
            inc[y] = c
            exc[y] = jnp.zeros_like(c)
            snd[k, 0, y] = c.astype(bf16)
            return 0

        lax.fori_loop(0, rows, row, 0, unroll=4)

    def scan(k):
        for s in range(hops):
            @pl.when(me + 2**s < n)
            def _():
                if s > 0:
                    snd[k, s] = inc[...].astype(bf16)
                scan_copy(k, s).start()

            @pl.when(me >= 2**s)
            def _():
                scan_copy(k, s).wait_recv()
                got = rcv[k, s].astype(f32)
                exc[...] += got
                if s + 1 < hops:
                    inc[...] += got

    def take_rim(k):
        for side, there in ((0, has_up), (1, has_down)):
            @pl.when(there)
            def _():
                rim_copy(k, side, me, False).wait_recv()
                expand(rim.at[k, side], 0 if side == 0 else rows + RIM, RIM)

    yes = me >= 0

    sent_state[0] = x[...].astype(bf16)
    send_rim(0, me, False, yes, True)

    @pl.when(me >= RETIRE)
    def _():
        z_copy().start()

    nexc[...] = jnp.zeros(nexc.shape, f32)
    ninc[0] = coef[0, 2] * z0[...]
    noise_send(0, 0)
    state[...] = x[...]

    @pl.when(jnp.logical_not(has_up))
    def _():
        st[pl.ds(0, RIM)] = jnp.zeros((RIM,) + st.shape[1:], bf16)

    @pl.when(jnp.logical_not(has_down))
    def _():
        st[pl.ds(rows + RIM, RIM)] = jnp.zeros((RIM,) + st.shape[1:], bf16)

    expand(x, RIM, rows)
    take_rim(0)
    network(0)
    finish(0, 0, z0)
    noise_advance(0, 0)
    scan(0)
    state[...] = x[...] + exc[...]
    sent_state[1] = state[...].astype(bf16)
    send_rim(1, me, False, yes, True)
    expand(state, RIM, rows)
    noise_advance(0, 1)

    @pl.when(me < stay)
    def _():
        z_copy().wait_recv()

    @pl.when(me >= stay)
    def _():
        z_arrived[...] = entrant[...]

    ninc[1] = coef[1, 2] * z_arrived[...]
    noise_send(1, 0)

    take_rim(1)
    network(0)
    finish(1, 0, None)
    scan(1)
    noise_finish(0, 2)
    state[...] = x[...] + (nexc[0] + exc[...])
    out[0] = state[...]

    sent_state[2] = state[...].astype(bf16)

    @pl.when(me >= RETIRE)
    def _():
        move_copy().start()

    send_rim(2, me - RETIRE, True, me >= RETIRE, True)
    send_rim(2, me, False, me >= stay, True)
    base_src[...] = state[...]

    @pl.when(me == RETIRE)
    def _():
        base[...] = base_src[...]
        for slot in range(n):
            if slot != RETIRE:
                base_copy(slot).start()

    noise_advance(1, 0)

    @pl.when(me < stay)
    def _():
        move_copy().wait_recv()
        state[...] = arrived[...].astype(f32)

    expand(state, RIM, rows)
    take_rim(2)
    network(1)
    finish(2, 1, z_arrived)
    scan(2)

    @pl.when(me != RETIRE)
    def _():
        base_copy(0).wait_recv()

    state[...] = base[...] + exc[...]
    sent_state[3] = state[...].astype(bf16)
    send_rim(3, me, False, yes, True)
    expand(state, RIM, rows)
    noise_advance(1, 1)
    take_rim(3)
    network(1)
    finish(3, 1, None)
    scan(3)
    noise_finish(1, 2)
    out[1] = base[...] + (nexc[1] + exc[...])

    for k, gate in ((0, yes), (1, yes), (2, me >= stay), (3, yes)):
        send_rim(k, me, False, gate, False)
    send_rim(2, me - RETIRE, True, me >= RETIRE, False)

    @pl.when(me >= RETIRE)
    def _():
        z_copy().wait_send()
        move_copy().wait_send()

    @pl.when(me == RETIRE)
    def _():
        for slot in range(n):
            if slot != RETIRE:
                base_copy(slot).wait_send()

    for s in range(hops):
        @pl.when(me + 2**s < n)
        def _():
            for k in range(4):
                scan_copy(k, s).wait_send()
            for k in range(2):
                nscan_copy(k, s).wait_send()


def shards(x_start, noise, fresh, sched, conv_in, conv_mid, conv_out, time_weight):
    slot, n, strips = lax.axis_index("tm"), lax.axis_size("tm"), lax.axis_size("rows")
    hidden, chans, rows, cols = conv_mid.shape[2], x_start.shape[1], x_start.shape[2], x_start.shape[3]
    hops = (n - 1).bit_length()
    table = plan_table(STEPS)
    spots = [lax.dynamic_slice_in_dim(sched, slot + RETIRE * r, 2, 0) for r in range(ROUNDS)]
    steps = jnp.stack(spots)
    logs = lookup(table, steps.reshape(-1)).reshape(ROUNDS, 2)
    coef = coefficients(logs[:, 0], logs[:, 1])
    features = time_features(steps[:, 0].astype(f32), hidden)
    embedding = jnp.dot(features, time_weight.astype(f32), precision=lax.Precision.HIGHEST)
    emb = jnp.broadcast_to(embedding[:, :, None], (ROUNDS, hidden, cols))
    pick = jnp.clip(slot - (n - RETIRE), 0, fresh.shape[0] - 1)
    entrant = lax.dynamic_index_in_dim(fresh, pick, 0, keepdims=False)[0].transpose(1, 0, 2)
    x = x_start[0].transpose(1, 0, 2)
    z = noise[0, 0].transpose(1, 0, 2)
    w_in = conv_in.transpose(2, 0, 1, 3).reshape(hidden, -1)
    w_mid = conv_mid.transpose(2, 0, 1, 3).reshape(hidden, -1)
    w_out = conv_out.reshape(-1, hidden)

    frame = (rows, chans, cols)
    vmem, dma = pltpu.VMEM, pltpu.SemaphoreType.DMA
    result = pl.pallas_call(
        functools.partial(kernel, n, strips, hops),
        out_shape=jax.ShapeDtypeStruct((ROUNDS,) + frame, f32),
        in_specs=[pl.BlockSpec(memory_space=pltpu.SMEM)] + [pl.BlockSpec(memory_space=pltpu.VMEM)] * 7,
        out_specs=pl.BlockSpec(memory_space=pltpu.VMEM),
        scratch_shapes=[
            vmem((rows + 2 * RIM, 3 * chans, cols), bf16),
            vmem((rows + 4, 3 * hidden, cols), bf16),
            vmem((rows + 2, 9 * chans, cols), f32),
            vmem(frame, f32),
            vmem(frame, f32),
            vmem(frame, f32),
            vmem((2,) + frame, f32),
            vmem((2,) + frame, f32),
            vmem(frame, f32),
            vmem(frame, f32),
            vmem((4,) + frame, bf16),
            vmem((4, 2, RIM, chans, cols), bf16),
            vmem(frame, bf16),
            vmem(frame, f32),
            vmem((4, hops) + frame, bf16),
            vmem((4, hops) + frame, bf16),
            vmem((2, hops) + frame, f32),
            vmem((2, hops) + frame, f32),
            dma((4, 2)),
            dma((4, 2)),
            dma((2,)),
            dma,
            dma,
            dma,
            dma,
            dma((4, hops)),
            dma((4, hops)),
            dma((2, hops)),
            dma((2, hops)),
            dma((n,)),
            dma,
        ],
        compiler_params=pltpu.CompilerParams(has_side_effects=True, vmem_limit_bytes=48 * 2**20),
        cost_estimate=pl.CostEstimate(
            flops=8 * rows * cols * 9 * hidden * (hidden + 2 * chans),
            bytes_accessed=4 * 2**20,
            transcendentals=8 * rows * cols * hidden,
        ),
    )(coef, x, z, entrant, emb, w_in, w_mid, w_out)
    return result.transpose(0, 2, 1, 3)[:, None, None]


def solution(mesh):
    placed = (
        P(None, None, "rows", None),
        P("tm", None, None, "rows", None),
        P(None, None, None, "rows", None),
        P(),
        P(),
        P(),
        P(),
        P(),
    )
    return jax.shard_map(
        shards,
        mesh=mesh,
        in_specs=placed,
        out_specs=P(None, "tm", None, None, "rows", None),
        check_vma=False,
    )
```

profile of v0, /device:TPU:25, one launch (start us, length us, event | category | flops | bytes accessed | tf_op | source)
XLA Modules:
  0.0 85.3 jit_solution(16771363103769168497)
XLA Ops:
  0.0 0.0 copy-start
  0.0 0.7 copy-done.6
  0.7 0.1 dynamic-slice_bitcast_fusion.1
  0.8 0.1 convert_reduce_fusion
  0.9 0.1 multiply_sine_fusion
  1.1 1.1 %fusion = f32[2,192]{1,0:T(2,128)S(1)} fusion(bf16[192,192]{1,0:T(8,128)(2,1)} %param.16, f32[2,96]{1,0:T(2,128)S(1)} %get-tuple-element.6, f32[2,96]{1,0:T(2,128)S(1)} %get-tuple-element.5), kind=kOutput, calls=%fused_computation.5 | convolution fusion | flops 885120 | bytes 76800 | tf_op jit(solution)/shard_map/dot_general | solution.py:366
  2.1 0.2 broadcast_in_dim.27.emb
  2.3 0.1 eq.16
  2.4 0.5 copy-done.5
  2.9 0.2 select_reduce_fusion
  3.1 0.1 reshape.22
  3.1 0.1 rsqrt_add_fusion
  3.2 0.1 pad_maximum_fusion.coef
  3.3 0.9 %copy-done.3 = f32[1,1,16,16,128]{4,3,2,1,0:T(8,128)S(1)} copy-done((f32[1,1,16,16,128]{4,3,2,1,0:T(8,128)S(1)}, f32[1,1,16,16,128]{4,3,2,1,0:T(8,128)}, u32[]{:S(2)}) %copy-start.3) | copy-done | bytes 131096
  4.2 0.1 copy_bitcast_fusion
  4.3 1.6 %copy.26 = bf16[192,3,3,192]{0,3,2,1:T(8,128)(2,1)S(1)} copy(bf16[192,3,3,192]{3,0,2,1:T(8,128)(2,1)} %bitcast.31) | data formatting | bytes 1327104 | tf_op jit(solution)/shard_map/transpose | solution.py:373
  5.9 0.0 copy-start.2
  5.9 0.3 copy.28.w_mid
  6.2 0.6 copy-done.2
  6.9 0.8 copy-done.4
  7.7 0.1 copy.27.w_in
  7.8 0.8 copy-done.1
  8.6 76.0 %shard_map.91 = f32[2,16,16,128]{3,2,1,0:T(8,128)S(1)} custom-call(f32[2,3]{1,0:T(2,128)S(1)} %pad_maximum_fusion.coef, f32[16,16,128]{2,1,0:T(8,128)S(1)} %bitcast.28, f32[16,16,128]{2,1,0:T(8,128)S(1)} %get-tuple-element.13.z0, f32[16,16,128]{2,1,0:T(8,128)S(1)} %get-tuple-element.12.entrant, f32[2,192,128]{2,1,0:T(8,128)S(1)} %broadcast_in_dim.27.emb, ...), custom_call_target="tpu_custom_call" | custom-call | flops 6341787648 | bytes 4194304 | tf_op jit(solution)/shard_map/pallas_call | solution.py:378
  84.6 0.8 copy.29
  (10 shorter events, 0.1 us)
Async XLA Ops:
  0.0 3.3 %copy-start = (f32[5,1,16,16,128]{4,3,2,1,0:T(8,128)S(1)}, f32[5,1,16,16,128]{4,3,2,1,0:T(8,128)}, u32[]{:S(2)}) copy-start(f32[5,1,16,16,128]{4,3,2,1,0:T(8,128)} %param.11) | copy-start | bytes 1966084
  0.0 0.7 copy-start.6
  2.1 0.7 copy-start.5
  3.3 0.9 %copy-start.3 = (f32[1,1,16,16,128]{4,3,2,1,0:T(8,128)S(1)}, f32[1,1,16,16,128]{4,3,2,1,0:T(8,128)}, u32[]{:S(2)}) copy-start(f32[1,1,16,16,128]{4,3,2,1,0:T(8,128)} %param.10) | copy-start | bytes 393220
  5.9 0.9 %copy-start.2 = (f32[1,16,16,128]{3,2,1,0:T(8,128)S(1)}, f32[1,16,16,128]{3,2,1,0:T(8,128)}, u32[]{:S(2)}) copy-start(f32[1,16,16,128]{3,2,1,0:T(8,128)} %param.9) | copy-start | bytes 393220
  6.8 0.9 %copy-start.4 = (bf16[3,3,192,16]{2,3,1,0:T(8,128)(2,1)S(1)}, bf16[3,3,192,16]{2,3,1,0:T(8,128)(2,1)}, u32[]{:S(2)}) copy-start(bf16[3,3,192,16]{2,3,1,0:T(8,128)(2,1)} %param.13) | copy-start | bytes 165892
  7.7 0.9 %copy-start.1 = (bf16[3,3,16,192]{3,2,1,0:T(8,128)(2,1)S(1)}, bf16[3,3,16,192]{3,2,1,0:T(8,128)(2,1)}, u32[]{:S(2)}) copy-start(bf16[3,3,16,192]{3,2,1,0:T(8,128)(2,1)} %param.15) | copy-start | bytes 165892
where the time goes:
time: 85.7 us; the launch traced here: 85.3 us
  Pallas kernels  76 us (89%)
  local copies, waits for them, and re-layouts  7.63 us (9%)
  matrix products  1.07 us (1%)
    pallas_call x1, Pallas kernels, shards(): pl.pallas_call(functools.partial(kernel, n, strips, hops), out_shape=jax....  76 us
    unnamed x15, local copies, waits for them, and re-layouts  4.37 us

commit v1 on v0

--- a/solution.py
+++ b/solution.py
@@ -64,17 +64,29 @@
 
 def kernel(
     n, strips, hops,
-    coef, x, z0, entrant, emb, w_in, w_mid, w_out, out,
+    coef, x_far, z_far, fresh_far, emb_far, in_far, mid_far, out_far, out,
+    x_raw, z_raw, fresh_raw, emb, in_raw, mid_raw, w_out, x, z0, w_in, w_mid,
     st, first, parts, state, exc, inc, nexc, ninc, base, base_src,
     sent_state, rim, arrived, z_arrived,
     snd, rcv, nsnd, nrcv,
     rim_ss, rim_rs, far_ss, mv_ss, mv_rs, z_ss, z_rs,
-    scan_ss, scan_rs, nscan_ss, nscan_rs, base_ss, base_rs,
+    scan_ss, scan_rs, nscan_ss, nscan_rs, base_ss, base_rs, load_s,
 ):
     me, strip = lax.axis_index("tm"), lax.axis_index("rows")
     rows, chans, cols = x.shape
     hidden = w_mid.shape[0]
+    half = rows // 2
     stay = n - RETIRE
+    pick = jnp.clip(me - stay, 0, fresh_far.shape[0] - 1)
+    loads = [
+        pltpu.make_async_copy(source, target, load_s.at[i])
+        for i, (source, target) in enumerate((
+            (x_far.at[0], x_raw), (in_far, in_raw), (emb_far, emb), (mid_far, mid_raw),
+            (out_far, w_out), (z_far.at[0, 0], z_raw), (fresh_far.at[pick, 0], fresh_raw),
+        ))
+    ]
+    for load in loads:
+        load.start()
     has_up, has_down = strip > 0, strip < strips - 1
 
     def remote(src, dst, ss, rs, slot, to_strip):
@@ -106,8 +118,35 @@
     def base_copy(slot):
         return remote(base_src, base, base_ss.at[slot], base_rs, slot, strip)
 
-    def scan_copy(k, s):
-        return remote(snd.at[k, s], rcv.at[k, s], scan_ss.at[k, s], scan_rs.at[k, s], me + 2**s, strip)
+    def scan_copy(k, s, part):
+        at = pl.ds(part * half, half)
+        return remote(
+            snd.at[k, s, at], rcv.at[k, s, at], scan_ss.at[k, s, part], scan_rs.at[k, s, part], me + 2**s, strip
+        )
+
+    def scan_send(k, s, part):
+        if s >= hops:
+            return
+
+        @pl.when(me + 2**s < n)
+        def _():
+            at = pl.ds(part * half, half)
+            if s > 0:
+                snd[k, s, at] = inc[at].astype(bf16)
+            scan_copy(k, s, part).start()
+
+    def scan_take(k, s, part):
+        if s >= hops:
+            return
+
+        @pl.when(me >= 2**s)
+        def _():
+            at = pl.ds(part * half, half)
+            scan_copy(k, s, part).wait_recv()
+            got = rcv[k, s, at].astype(f32)
+            exc[at] += got
+            if s + 1 < hops:
+                inc[at] += got
 
     def nscan_copy(k, s):
         return remote(nsnd.at[k, s], nrcv.at[k, s], nscan_ss.at[k, s], nscan_rs.at[k, s], me + 2**s, strip)
@@ -143,57 +182,43 @@
         for t in range(s, hops):
             noise_advance(k, t)
 
-    def network(r):
-        embedding = emb.at[r]
-
-        def in_step(i, _):
+    def sweep(k, r, noise):
+        keep, predict, spread = coef[r, 0], coef[r, 1], coef[r, 2]
+        up_scale, down_scale = has_up.astype(f32), has_down.astype(f32)
+        in_steps, mid_steps = (rows + 4) // 2, (rows + 2) // 2
+
+        def in_step(i):
             f = 2 * i
             both = jnp.concatenate(
-                [st[pl.ds(f + t, 3)].reshape(9 * chans, cols) for t in range(2)], axis=1
+                [st[f + t : f + t + 3].reshape(9 * chans, cols) for t in range(2)], axis=1
             )
             h = jnp.dot(w_in[...], both, preferred_element_type=f32)
             for t in range(2):
-                v = silu(h[:, t * cols : (t + 1) * cols] + embedding[...])
+                v = silu(h[:, t * cols : (t + 1) * cols] + emb[r])
+                if i == 0:
+                    v = v * up_scale
+                if i == in_steps - 1:
+                    v = v * down_scale
                 first[f + t] = spread_rows(v)
-            return 0
-
-        lax.fori_loop(0, (rows + 4) // 2, in_step, 0, unroll=2)
-
-        @pl.when(jnp.logical_not(has_up))
-        def _():
-            first[pl.ds(0, 2)] = jnp.zeros((2,) + first.shape[1:], bf16)
-
-        @pl.when(jnp.logical_not(has_down))
-        def _():
-            first[pl.ds(rows + 2, 2)] = jnp.zeros((2,) + first.shape[1:], bf16)
-
-        def mid_step(i, _):
+
+        def mid_step(i):
             f = 2 * i
             both = jnp.concatenate(
-                [first[pl.ds(f + t, 3)].reshape(9 * hidden, cols) for t in range(2)], axis=1
+                [first[f + t : f + t + 3].reshape(9 * hidden, cols) for t in range(2)], axis=1
             )
             g = silu(jnp.dot(w_mid[...], both, preferred_element_type=f32)).astype(bf16)
             p = jnp.dot(w_out[...], g, preferred_element_type=f32)
             for t in range(2):
-                parts[f + t] = p[:, t * cols : (t + 1) * cols]
-            return 0
-
-        lax.fori_loop(0, (rows + 2) // 2, mid_step, 0, unroll=3)
-
-        @pl.when(jnp.logical_not(has_up))
-        def _():
-            parts[0] = jnp.zeros(parts.shape[1:], f32)
-
-        @pl.when(jnp.logical_not(has_down))
-        def _():
-            parts[rows + 1] = jnp.zeros(parts.shape[1:], f32)
-
-    def finish(k, r, noise):
-        keep, predict, spread = coef[r, 0], coef[r, 1], coef[r, 2]
-
-        def row(y, _):
+                v = p[:, t * cols : (t + 1) * cols]
+                if f + t == 0:
+                    v = v * up_scale
+                if f + t == rows + 1:
+                    v = v * down_scale
+                parts[f + t] = v
+
+        def finish(y):
             sums = [
-                sum(parts[y + a, pl.ds((3 * a + b) * chans, chans)] for a in range(3))
+                sum(parts[y + a, (3 * a + b) * chans : (3 * a + b + 1) * chans] for a in range(3))
                 for b in range(3)
             ]
             predicted = moved_right(sums[0]) + sums[1] + moved_left(sums[2])
@@ -203,25 +228,29 @@
             inc[y] = c
             exc[y] = jnp.zeros_like(c)
             snd[k, 0, y] = c.astype(bf16)
-            return 0
-
-        lax.fori_loop(0, rows, row, 0, unroll=4)
-
-    def scan(k):
+
+        in_step(0)
+        in_step(1)
+        sent_at = half // 2
+        for i in range(mid_steps):
+            if i + 2 < in_steps:
+                in_step(i + 2)
+            mid_step(i)
+            if i > 0:
+                finish(2 * i - 2)
+                finish(2 * i - 1)
+            if i == sent_at:
+                scan_send(k, 0, 0)
+            if i == sent_at + 2:
+                scan_take(k, 0, 0)
+                scan_send(k, 1, 0)
+        scan_send(k, 0, 1)
         for s in range(hops):
-            @pl.when(me + 2**s < n)
-            def _():
-                if s > 0:
-                    snd[k, s] = inc[...].astype(bf16)
-                scan_copy(k, s).start()
-
-            @pl.when(me >= 2**s)
-            def _():
-                scan_copy(k, s).wait_recv()
-                got = rcv[k, s].astype(f32)
-                exc[...] += got
-                if s + 1 < hops:
-                    inc[...] += got
+            if s > 0:
+                scan_take(k, s, 0)
+                scan_send(k, s + 1, 0)
+            scan_take(k, s, 1)
+            scan_send(k, s + 1, 1)
 
     def take_rim(k):
         for side, there in ((0, has_up), (1, has_down)):
@@ -232,8 +261,12 @@
 
     yes = me >= 0
 
+    loads[0].wait()
+    x[...] = jnp.swapaxes(x_raw[...], 0, 1)
     sent_state[0] = x[...].astype(bf16)
     send_rim(0, me, False, yes, True)
+    loads[5].wait()
+    z0[...] = jnp.swapaxes(z_raw[...], 0, 1)
 
     @pl.when(me >= RETIRE)
     def _():
@@ -253,11 +286,14 @@
         st[pl.ds(rows + RIM, RIM)] = jnp.zeros((RIM,) + st.shape[1:], bf16)
 
     expand(x, RIM, rows)
+    for i in (1, 2, 3, 4, 6):
+        loads[i].wait()
+    taps = [(a, b) for a in range(3) for b in range(3)]
+    w_in[...] = in_raw[...].astype(f32).T.astype(bf16)
+    w_mid[...] = jnp.concatenate([mid_raw[a, b] for a, b in taps], axis=1)
     take_rim(0)
-    network(0)
-    finish(0, 0, z0)
+    sweep(0, 0, z0)
     noise_advance(0, 0)
-    scan(0)
     state[...] = x[...] + exc[...]
     sent_state[1] = state[...].astype(bf16)
     send_rim(1, me, False, yes, True)
@@ -270,15 +306,13 @@
 
     @pl.when(me >= stay)
     def _():
-        z_arrived[...] = entrant[...]
+        z_arrived[...] = jnp.swapaxes(fresh_raw[...], 0, 1)
 
     ninc[1] = coef[1, 2] * z_arrived[...]
     noise_send(1, 0)
 
     take_rim(1)
-    network(0)
-    finish(1, 0, None)
-    scan(1)
+    sweep(1, 0, None)
     noise_finish(0, 2)
     state[...] = x[...] + (nexc[0] + exc[...])
     out[0] = state[...]
@@ -309,9 +343,7 @@
 
     expand(state, RIM, rows)
     take_rim(2)
-    network(1)
-    finish(2, 1, z_arrived)
-    scan(2)
+    sweep(2, 1, z_arrived)
 
     @pl.when(me != RETIRE)
     def _():
@@ -323,9 +355,7 @@
     expand(state, RIM, rows)
     noise_advance(1, 1)
     take_rim(3)
-    network(1)
-    finish(3, 1, None)
-    scan(3)
+    sweep(3, 1, None)
     noise_finish(1, 2)
     out[1] = base[...] + (nexc[1] + exc[...])
 
@@ -348,7 +378,8 @@
         @pl.when(me + 2**s < n)
         def _():
             for k in range(4):
-                scan_copy(k, s).wait_send()
+                scan_copy(k, s, 0).wait_send()
+                scan_copy(k, s, 1).wait_send()
             for k in range(2):
                 nscan_copy(k, s).wait_send()
 
@@ -365,22 +396,25 @@
     features = time_features(steps[:, 0].astype(f32), hidden)
     embedding = jnp.dot(features, time_weight.astype(f32), precision=lax.Precision.HIGHEST)
     emb = jnp.broadcast_to(embedding[:, :, None], (ROUNDS, hidden, cols))
-    pick = jnp.clip(slot - (n - RETIRE), 0, fresh.shape[0] - 1)
-    entrant = lax.dynamic_index_in_dim(fresh, pick, 0, keepdims=False)[0].transpose(1, 0, 2)
-    x = x_start[0].transpose(1, 0, 2)
-    z = noise[0, 0].transpose(1, 0, 2)
-    w_in = conv_in.transpose(2, 0, 1, 3).reshape(hidden, -1)
-    w_mid = conv_mid.transpose(2, 0, 1, 3).reshape(hidden, -1)
-    w_out = conv_out.reshape(-1, hidden)
-
     frame = (rows, chans, cols)
     vmem, dma = pltpu.VMEM, pltpu.SemaphoreType.DMA
     result = pl.pallas_call(
         functools.partial(kernel, n, strips, hops),
         out_shape=jax.ShapeDtypeStruct((ROUNDS,) + frame, f32),
-        in_specs=[pl.BlockSpec(memory_space=pltpu.SMEM)] + [pl.BlockSpec(memory_space=pltpu.VMEM)] * 7,
+        in_specs=[pl.BlockSpec(memory_space=pltpu.SMEM)] + [pl.BlockSpec(memory_space=pltpu.HBM)] * 7,
         out_specs=pl.BlockSpec(memory_space=pltpu.VMEM),
         scratch_shapes=[
+            vmem((chans, rows, cols), f32),
+            vmem((chans, rows, cols), f32),
+            vmem((chans, rows, cols), f32),
+            vmem((ROUNDS, hidden, cols), f32),
+            vmem((9 * chans, hidden), bf16),
+            vmem(conv_mid.shape, bf16),
+            vmem((9 * chans, hidden), bf16),
+            vmem(frame, f32),
+            vmem(frame, f32),
+            vmem((hidden, 9 * chans), bf16),
+            vmem((hidden, 9 * hidden), bf16),
             vmem((rows + 2 * RIM, 3 * chans, cols), bf16),
             vmem((rows + 4, 3 * hidden, cols), bf16),
             vmem((rows + 2, 9 * chans, cols), f32),
@@ -406,20 +440,21 @@
             dma,
             dma,
             dma,
-            dma((4, hops)),
-            dma((4, hops)),
+            dma((4, hops, 2)),
+            dma((4, hops, 2)),
             dma((2, hops)),
             dma((2, hops)),
             dma((n,)),
             dma,
+            dma((7,)),
         ],
-        compiler_params=pltpu.CompilerParams(has_side_effects=True, vmem_limit_bytes=48 * 2**20),
+        compiler_params=pltpu.CompilerParams(has_side_effects=True, vmem_limit_bytes=56 * 2**20),
         cost_estimate=pl.CostEstimate(
             flops=8 * rows * cols * 9 * hidden * (hidden + 2 * chans),
             bytes_accessed=4 * 2**20,
             transcendentals=8 * rows * cols * hidden,
         ),
-    )(coef, x, z, entrant, emb, w_in, w_mid, w_out)
+    )(coef, x_start, noise, fresh, emb, conv_in.transpose(0, 1, 3, 2).reshape(-1, hidden), conv_mid, conv_out.reshape(-1, hidden))
     return result.transpose(0, 2, 1, 3)[:, None, None]
 
 

time: 85.7 us -> 87.3 us (1.019)
  Pallas kernels: 76 us -> 80.7 us
  local copies, waits for them, and re-layouts: 7.63 us -> 3.94 us
  matrix products: 1.07 us -> 0.18 us
    pallas_call x1, Pallas kernels: 76 us -> 80.7 us  [shards(): pl.pallas_call(functools.partial(kernel, n, strips, hops), out_shape=jax....]
    unnamed x15 -> x6, local copies, waits for them, and re-layouts: 4.37 us -> 1.17 us
    transpose x2 -> x0, local copies, waits for them, and re-layouts: 1.68 us -> none  [the longest x1 1.6 us: shards(): w_mid = conv_mid.transpose(2, 0, 1, 3).reshape(hidden, -1)]
    broadcast_in_dim x1, local copies, waits for them, and re-layouts: 0.78 us -> 1.73 us  [shards(): return result.transpose(0, 2, 1, 3)[:, None, None]]
    dot_general x1, matrix products: 1.07 us -> 0.18 us  [shards(): jnp.dot(features, time_weight.astype(f32), precision=lax.Precision.HIGHEST)]
where the time goes in v1:
time: 87.3 us; the launch traced here: 86.1 us
  Pallas kernels  80.7 us (92%)
  local copies, waits for them, and re-layouts  3.94 us (5%)
  other arithmetic  1.22 us (1%)
    pallas_call x1, Pallas kernels, shards(): pl.pallas_call(functools.partial(kernel, n, strips, hops), out_shape=jax....  80.7 us

profile of v1, /device:TPU:25, one launch (start us, length us, event | category | flops | bytes accessed | tf_op | source)
XLA Modules:
  0.0 86.1 jit_solution(10951050512443623930)
XLA Ops:
  0.0 0.0 copy-start
  0.0 0.0 copy-start.2
  0.0 0.7 copy-done.2
  0.7 0.1 dynamic-slice_bitcast_fusion.1
  0.8 0.0 copy-start.1
  0.8 0.1 convert_reduce_fusion
  0.9 0.1 eq.16
  1.0 0.5 copy-done.1
  1.5 0.2 select_reduce_fusion
  1.6 0.1 reshape.18
  1.7 0.1 multiply_sine_fusion
  1.9 0.0 copy-done
  1.9 0.2 fusion
  2.0 0.1 rsqrt_add_fusion
  2.2 0.7 pad_maximum_fusion.coef
  2.8 0.8 broadcast_in_dim.27.emb_far
  3.6 80.7 %shard_map.91 = f32[2,16,16,128]{3,2,1,0:T(8,128)} custom-call(f32[2,3]{1,0:T(2,128)} %pad_maximum_fusion.coef, f32[1,16,16,128]{3,2,1,0:T(8,128)} %x_far.1, f32[1,1,16,16,128]{4,3,2,1,0:T(8,128)} %z_far.1, f32[5,1,16,16,128]{4,3,2,1,0:T(8,128)} %fresh_far.1, f32[2,192,128]{2,1,0:T(8,128)} %broadcast_in_dim.27.emb_far, bf16[144,192]{1,0:T(8,128)(2,1)} %bitcast.13, ...), custom_call_target="tpu_custom_call" | custom-call | flops 6341787648 | bytes 4194304 | tf_op jit(solution)/shard_map/pallas_call | solution.py:401
  84.4 1.7 %copy.12 = f32[2,1,1,16,16,128]{5,4,3,2,1,0:T(8,128)} copy(f32[2,1,1,16,16,128]{5,3,4,0,2,1:T(8,128)} %bitcast.12) | data formatting | bytes 524288 | tf_op jit(solution)/shard_map/broadcast_in_dim | solution.py:458
  (2 shorter events, 0.0 us)
Async XLA Ops:
  0.0 1.9 %copy-start = (bf16[192,192]{1,0:T(8,128)(2,1)S(1)}, bf16[192,192]{1,0:T(8,128)(2,1)}, u32[]{:S(2)}) copy-start(bf16[192,192]{1,0:T(8,128)(2,1)} %param.16) | copy-start | bytes 221188
  0.0 0.7 copy-start.2
  0.8 0.7 copy-start.1

commit v2 on v1

--- a/solution.py
+++ b/solution.py
@@ -64,9 +64,9 @@
 
 def kernel(
     n, strips, hops,
-    coef, x_far, z_far, fresh_far, emb_far, in_far, mid_far, out_far, out,
-    x_raw, z_raw, fresh_raw, emb, in_raw, mid_raw, w_out, x, z0, w_in, w_mid,
-    st, first, parts, state, exc, inc, nexc, ninc, base, base_src,
+    coef, x_far, z_far, fresh_far, emb, in_far, mid_far, out_far, out,
+    x_raw, z_raw, fresh_raw, in_raw, mid_raw, w_out, x, z0, w_in, w_mid,
+    st, first, parts, state, exc, inc, nexc, ninc, base,
     sent_state, rim, arrived, z_arrived,
     snd, rcv, nsnd, nrcv,
     rim_ss, rim_rs, far_ss, mv_ss, mv_rs, z_ss, z_rs,
@@ -81,7 +81,7 @@
     loads = [
         pltpu.make_async_copy(source, target, load_s.at[i])
         for i, (source, target) in enumerate((
-            (x_far.at[0], x_raw), (in_far, in_raw), (emb_far, emb), (mid_far, mid_raw),
+            (x_far.at[0], x_raw), (in_far, in_raw), (mid_far, mid_raw),
             (out_far, w_out), (z_far.at[0, 0], z_raw), (fresh_far.at[pick, 0], fresh_raw),
         ))
     ]
@@ -115,8 +115,26 @@
     def z_copy():
         return remote(z0, z_arrived, z_ss, z_rs, me - RETIRE, strip)
 
-    def base_copy(slot):
-        return remote(base_src, base, base_ss.at[slot], base_rs, slot, strip)
+    def base_copy(to, lane):
+        return remote(base, base, base_ss.at[lane], base_rs, to, strip)
+
+    mate = RETIRE + 1 - 2 * (RETIRE % 2)
+    low, high = min(RETIRE, mate), max(RETIRE, mate)
+    base_moves = (
+        (me == RETIRE, mate, 0),
+        (jnp.logical_and(me <= high, me >= 2), me - 2, 1),
+        (jnp.logical_and(me >= low, me + 2 < n), me + 2, 2),
+    )
+
+    def base_pass(gate):
+        @pl.when(jnp.logical_and(gate, me != RETIRE))
+        def _():
+            base_copy(me, 0).wait_recv()
+
+        for allowed, to, lane in base_moves:
+            @pl.when(jnp.logical_and(gate, allowed))
+            def _():
+                base_copy(to, lane).start()
 
     def scan_copy(k, s, part):
         at = pl.ds(part * half, half)
@@ -148,8 +166,11 @@
             if s + 1 < hops:
                 inc[at] += got
 
+    level, odd = me // 2, me % 2
+
     def nscan_copy(k, s):
-        return remote(nsnd.at[k, s], nrcv.at[k, s], nscan_ss.at[k, s], nscan_rs.at[k, s], me + 2**s, strip)
+        to = me + 1 - 2 * odd if s == 0 else me + 2
+        return remote(nsnd.at[k, s], nrcv.at[k, s], nscan_ss.at[k, s], nscan_rs.at[k, s], to, strip)
 
     def spread_rows(v):
         v = v.astype(f32)
@@ -159,30 +180,28 @@
         for i in range(count):
             st[at + i] = spread_rows(source[i])
 
-    def noise_send(k, s):
-        @pl.when(me + 2**s < n)
-        def _():
-            nsnd[k, s] = ninc[k]
-            nscan_copy(k, s).start()
-
-    def noise_take(k, s):
-        @pl.when(me >= 2**s)
-        def _():
-            nscan_copy(k, s).wait_recv()
-            nexc[k] += nrcv[k, s]
-            ninc[k] += nrcv[k, s]
-
-    def noise_advance(k, s):
-        if s < hops:
-            noise_take(k, s)
-        if s + 1 < hops:
-            noise_send(k, s + 1)
-
-    def noise_finish(k, s):
-        for t in range(s, hops):
-            noise_advance(k, t)
-
-    def sweep(k, r, noise):
+    def noise_start(k, z):
+        nsnd[k, 0] = coef[k, 2] * z[...]
+        nscan_copy(k, 0).start()
+
+    def noise_pair(k):
+        nscan_copy(k, 0).wait_recv()
+        ninc[k] = nsnd[k, 0] + nrcv[k, 0]
+        nexc[k] = nrcv[k, 0] * odd.astype(f32)
+
+    def noise_pass(k, gate):
+        @pl.when(jnp.logical_and(gate, level > 0))
+        def _():
+            nscan_copy(k, 1).wait_recv()
+            nexc[k] += nrcv[k, 1]
+            ninc[k] += nrcv[k, 1]
+
+        @pl.when(jnp.logical_and(gate, me + 2 < n))
+        def _():
+            nsnd[k, 1] = ninc[k]
+            nscan_copy(k, 1).start()
+
+    def sweep(k, r, noise, hooks=()):
         keep, predict, spread = coef[r, 0], coef[r, 1], coef[r, 2]
         up_scale, down_scale = has_up.astype(f32), has_down.astype(f32)
         in_steps, mid_steps = (rows + 4) // 2, (rows + 2) // 2
@@ -241,6 +260,9 @@
                 finish(2 * i - 1)
             if i == sent_at:
                 scan_send(k, 0, 0)
+            for at, hook in hooks:
+                if i == at:
+                    hook()
             if i == sent_at + 2:
                 scan_take(k, 0, 0)
                 scan_send(k, 1, 0)
@@ -260,21 +282,20 @@
                 expand(rim.at[k, side], 0 if side == 0 else rows + RIM, RIM)
 
     yes = me >= 0
+    early, late = 2, rows // 2 - 1
 
     loads[0].wait()
     x[...] = jnp.swapaxes(x_raw[...], 0, 1)
     sent_state[0] = x[...].astype(bf16)
     send_rim(0, me, False, yes, True)
-    loads[5].wait()
+    loads[4].wait()
     z0[...] = jnp.swapaxes(z_raw[...], 0, 1)
 
     @pl.when(me >= RETIRE)
     def _():
         z_copy().start()
 
-    nexc[...] = jnp.zeros(nexc.shape, f32)
-    ninc[0] = coef[0, 2] * z0[...]
-    noise_send(0, 0)
+    noise_start(0, z0)
     state[...] = x[...]
 
     @pl.when(jnp.logical_not(has_up))
@@ -286,19 +307,22 @@
         st[pl.ds(rows + RIM, RIM)] = jnp.zeros((RIM,) + st.shape[1:], bf16)
 
     expand(x, RIM, rows)
-    for i in (1, 2, 3, 4, 6):
+    for i in (1, 2, 3, 5):
         loads[i].wait()
     taps = [(a, b) for a in range(3) for b in range(3)]
     w_in[...] = in_raw[...].astype(f32).T.astype(bf16)
     w_mid[...] = jnp.concatenate([mid_raw[a, b] for a, b in taps], axis=1)
     take_rim(0)
-    sweep(0, 0, z0)
-    noise_advance(0, 0)
+    def first_pairs():
+        noise_pair(0)
+        noise_pass(0, level == 0)
+
+    sweep(0, 0, z0, ((early, first_pairs),))
     state[...] = x[...] + exc[...]
     sent_state[1] = state[...].astype(bf16)
     send_rim(1, me, False, yes, True)
     expand(state, RIM, rows)
-    noise_advance(0, 1)
+    noise_pass(0, level == 1)
 
     @pl.when(me < stay)
     def _():
@@ -308,12 +332,16 @@
     def _():
         z_arrived[...] = jnp.swapaxes(fresh_raw[...], 0, 1)
 
-    ninc[1] = coef[1, 2] * z_arrived[...]
-    noise_send(1, 0)
+    noise_start(1, z_arrived)
 
     take_rim(1)
-    sweep(1, 0, None)
-    noise_finish(0, 2)
+    def second_pairs():
+        noise_pass(0, level == 2)
+        noise_pair(1)
+        noise_pass(1, level == 0)
+
+    sweep(1, 0, None, ((early, second_pairs),))
+    noise_pass(0, level >= 3)
     state[...] = x[...] + (nexc[0] + exc[...])
     out[0] = state[...]
 
@@ -325,16 +353,13 @@
 
     send_rim(2, me - RETIRE, True, me >= RETIRE, True)
     send_rim(2, me, False, me >= stay, True)
-    base_src[...] = state[...]
 
     @pl.when(me == RETIRE)
     def _():
-        base[...] = base_src[...]
-        for slot in range(n):
-            if slot != RETIRE:
-                base_copy(slot).start()
-
-    noise_advance(1, 0)
+        base[...] = state[...]
+
+    base_pass(me == RETIRE)
+    noise_pass(1, level == 1)
 
     @pl.when(me < stay)
     def _():
@@ -343,20 +368,23 @@
 
     expand(state, RIM, rows)
     take_rim(2)
-    sweep(2, 1, z_arrived)
-
-    @pl.when(me != RETIRE)
-    def _():
-        base_copy(0).wait_recv()
-
+    near = jnp.logical_or(me == mate, me == RETIRE - 2)
+    next_near = me == mate - 2
+
+    def base_far():
+        base_pass(next_near)
+        noise_pass(1, level == 2)
+
+    sweep(2, 1, z_arrived, ((early, lambda: base_pass(near)), (late, base_far)))
+
+    base_pass(jnp.logical_not(jnp.logical_or(me == RETIRE, jnp.logical_or(near, next_near))))
     state[...] = base[...] + exc[...]
     sent_state[3] = state[...].astype(bf16)
     send_rim(3, me, False, yes, True)
     expand(state, RIM, rows)
-    noise_advance(1, 1)
     take_rim(3)
     sweep(3, 1, None)
-    noise_finish(1, 2)
+    noise_pass(1, level >= 3)
     out[1] = base[...] + (nexc[1] + exc[...])
 
     for k, gate in ((0, yes), (1, yes), (2, me >= stay), (3, yes)):
@@ -368,11 +396,17 @@
         z_copy().wait_send()
         move_copy().wait_send()
 
-    @pl.when(me == RETIRE)
-    def _():
-        for slot in range(n):
-            if slot != RETIRE:
-                base_copy(slot).wait_send()
+    for allowed, to, lane in base_moves:
+        @pl.when(allowed)
+        def _():
+            base_copy(to, lane).wait_send()
+
+    for k in range(2):
+        nscan_copy(k, 0).wait_send()
+
+        @pl.when(me + 2 < n)
+        def _():
+            nscan_copy(k, 1).wait_send()
 
     for s in range(hops):
         @pl.when(me + 2**s < n)
@@ -380,8 +414,6 @@
             for k in range(4):
                 scan_copy(k, s, 0).wait_send()
                 scan_copy(k, s, 1).wait_send()
-            for k in range(2):
-                nscan_copy(k, s).wait_send()
 
 
 def shards(x_start, noise, fresh, sched, conv_in, conv_mid, conv_out, time_weight):
@@ -401,13 +433,14 @@
     result = pl.pallas_call(
         functools.partial(kernel, n, strips, hops),
         out_shape=jax.ShapeDtypeStruct((ROUNDS,) + frame, f32),
-        in_specs=[pl.BlockSpec(memory_space=pltpu.SMEM)] + [pl.BlockSpec(memory_space=pltpu.HBM)] * 7,
+        in_specs=[pl.BlockSpec(memory_space=pltpu.SMEM)] + [
+            pl.BlockSpec(memory_space=pltpu.VMEM if i == 3 else pltpu.HBM) for i in range(7)
+        ],
         out_specs=pl.BlockSpec(memory_space=pltpu.VMEM),
         scratch_shapes=[
             vmem((chans, rows, cols), f32),
             vmem((chans, rows, cols), f32),
             vmem((chans, rows, cols), f32),
-            vmem((ROUNDS, hidden, cols), f32),
             vmem((9 * chans, hidden), bf16),
             vmem(conv_mid.shape, bf16),
             vmem((9 * chans, hidden), bf16),
@@ -424,15 +457,14 @@
             vmem((2,) + frame, f32),
             vmem((2,) + frame, f32),
             vmem(frame, f32),
-            vmem(frame, f32),
             vmem((4,) + frame, bf16),
             vmem((4, 2, RIM, chans, cols), bf16),
             vmem(frame, bf16),
             vmem(frame, f32),
             vmem((4, hops) + frame, bf16),
             vmem((4, hops) + frame, bf16),
-            vmem((2, hops) + frame, f32),
-            vmem((2, hops) + frame, f32),
+            vmem((2, 2) + frame, f32),
+            vmem((2, 2) + frame, f32),
             dma((4, 2)),
             dma((4, 2)),
             dma((2,)),
@@ -442,11 +474,11 @@
             dma,
             dma((4, hops, 2)),
             dma((4, hops, 2)),
-            dma((2, hops)),
-            dma((2, hops)),
-            dma((n,)),
+            dma((2, 2)),
+            dma((2, 2)),
+            dma((3,)),
             dma,
-            dma((7,)),
+            dma((6,)),
         ],
         compiler_params=pltpu.CompilerParams(has_side_effects=True, vmem_limit_bytes=56 * 2**20),
         cost_estimate=pl.CostEstimate(

time: 87.3 us -> 81 us (0.928)
  Pallas kernels: 80.7 us -> 75 us
    pallas_call x1, Pallas kernels: 80.7 us -> 75 us  [shards(): pl.pallas_call(functools.partial(kernel, n, strips, hops), out_shape=jax....]
where the time goes in v2:
time: 81 us; the launch traced here: 80.4 us
  Pallas kernels  75 us (93%)
  local copies, waits for them, and re-layouts  3.94 us (5%)
  other arithmetic  1.22 us (2%)
    pallas_call x1, Pallas kernels, shards(): pl.pallas_call(functools.partial(kernel, n, strips, hops), out_shape=jax....  75 us
    broadcast_in_dim x1, local copies, waits for them, and re-layouts, shards(): return result.transpose(0, 2, 1, 3)[:, None, None]  1.73 us

profile of v2, /device:TPU:25, one launch (start us, length us, event | category | flops | bytes accessed | tf_op | source)
XLA Modules:
  0.0 80.4 jit_solution(1349753519295766950)
XLA Ops:
  0.0 0.0 copy-start
  0.0 0.0 copy-start.2
  0.0 0.7 copy-done.2
  0.7 0.1 dynamic-slice_bitcast_fusion.1
  0.8 0.0 copy-start.1
  0.8 0.1 convert_reduce_fusion
  0.9 0.1 eq.16
  1.0 0.5 copy-done.1
  1.5 0.2 select_reduce_fusion
  1.6 0.1 reshape.18
  1.7 0.1 multiply_sine_fusion
  1.9 0.0 copy-done
  1.9 0.2 fusion
  2.0 0.1 rsqrt_add_fusion
  2.2 0.7 pad_maximum_fusion.coef
  2.8 0.8 broadcast_in_dim.27.emb
  3.6 75.0 %shard_map.91 = f32[2,16,16,128]{3,2,1,0:T(8,128)} custom-call(f32[2,3]{1,0:T(2,128)} %pad_maximum_fusion.coef, f32[1,16,16,128]{3,2,1,0:T(8,128)} %x_far.1, f32[1,1,16,16,128]{4,3,2,1,0:T(8,128)} %z_far.1, f32[5,1,16,16,128]{4,3,2,1,0:T(8,128)} %fresh_far.1, f32[2,192,128]{2,1,0:T(8,128)} %broadcast_in_dim.27.emb, bf16[144,192]{1,0:T(8,128)(2,1)} %bitcast.13, ...), custom_call_target="tpu_custom_call" | custom-call | flops 6341787648 | bytes 4194304 | tf_op jit(solution)/shard_map/pallas_call | solution.py:433
  78.7 1.7 %copy.12 = f32[2,1,1,16,16,128]{5,4,3,2,1,0:T(8,128)} copy(f32[2,1,1,16,16,128]{5,3,4,0,2,1:T(8,128)} %bitcast.12) | data formatting | bytes 524288 | tf_op jit(solution)/shard_map/broadcast_in_dim | solution.py:490
  (2 shorter events, 0.0 us)
Async XLA Ops:
  0.0 1.9 %copy-start = (bf16[192,192]{1,0:T(8,128)(2,1)S(1)}, bf16[192,192]{1,0:T(8,128)(2,1)}, u32[]{:S(2)}) copy-start(bf16[192,192]{1,0:T(8,128)(2,1)} %param.16) | copy-start | bytes 221188
  0.0 0.7 copy-start.2
  0.8 0.7 copy-start.1

commit v3 on v2

--- a/solution.py
+++ b/solution.py
@@ -66,7 +66,7 @@
     n, strips, hops,
     coef, x_far, z_far, fresh_far, emb, in_far, mid_far, out_far, out,
     x_raw, z_raw, fresh_raw, in_raw, mid_raw, w_out, x, z0, w_in, w_mid,
-    st, first, parts, state, exc, inc, nexc, ninc, base,
+    st, first, middle, parts, state, exc, inc, nexc, ninc, base,
     sent_state, rim, arrived, z_arrived,
     snd, rcv, nsnd, nrcv,
     rim_ss, rim_rs, far_ss, mv_ss, mv_rs, z_ss, z_rs,
@@ -206,34 +206,30 @@
         up_scale, down_scale = has_up.astype(f32), has_down.astype(f32)
         in_steps, mid_steps = (rows + 4) // 2, (rows + 2) // 2
 
-        def in_step(i):
+        def in_step(i, scale=None):
             f = 2 * i
             both = jnp.concatenate(
-                [st[f + t : f + t + 3].reshape(9 * chans, cols) for t in range(2)], axis=1
+                [st[pl.ds(f + t, 3)].reshape(9 * chans, cols) for t in range(2)], axis=1
             )
             h = jnp.dot(w_in[...], both, preferred_element_type=f32)
             for t in range(2):
                 v = silu(h[:, t * cols : (t + 1) * cols] + emb[r])
-                if i == 0:
-                    v = v * up_scale
-                if i == in_steps - 1:
-                    v = v * down_scale
+                if scale is not None:
+                    v = v * scale
                 first[f + t] = spread_rows(v)
 
         def mid_step(i):
             f = 2 * i
             both = jnp.concatenate(
-                [first[f + t : f + t + 3].reshape(9 * hidden, cols) for t in range(2)], axis=1
+                [first[pl.ds(f + t, 3)].reshape(9 * hidden, cols) for t in range(2)], axis=1
             )
-            g = silu(jnp.dot(w_mid[...], both, preferred_element_type=f32)).astype(bf16)
+            middle[...] = jnp.dot(w_mid[...], both, preferred_element_type=f32)
+
+        def out_step(i):
+            g = silu(middle[...]).astype(bf16)
             p = jnp.dot(w_out[...], g, preferred_element_type=f32)
-            for t in range(2):
-                v = p[:, t * cols : (t + 1) * cols]
-                if f + t == 0:
-                    v = v * up_scale
-                if f + t == rows + 1:
-                    v = v * down_scale
-                parts[f + t] = v
+            parts[2 * i] = p[:, :cols] * jnp.where(i == 0, up_scale, 1.0)
+            parts[2 * i + 1] = p[:, cols:] * jnp.where(i == mid_steps - 1, down_scale, 1.0)
 
         def finish(y):
             sums = [
@@ -248,29 +244,27 @@
             exc[y] = jnp.zeros_like(c)
             snd[k, 0, y] = c.astype(bf16)
 
-        in_step(0)
+        def step(i, _):
+            for t in range(2):
+                finish(jnp.maximum(2 * i - 6 + t, 0))
+            out_step(jnp.maximum(i - 1, 0))
+            mid_step(i)
+            in_step(i + 2, jnp.where(i + 2 == in_steps - 1, down_scale, 1.0))
+            for at, hook in hooks:
+                pl.when(i == at)(hook)
+            pl.when(i == half // 2 + 2)(lambda: scan_send(k, 0, 0))
+            return 0
+
+        in_step(0, up_scale)
         in_step(1)
-        sent_at = half // 2
-        for i in range(mid_steps):
-            if i + 2 < in_steps:
-                in_step(i + 2)
-            mid_step(i)
-            if i > 0:
-                finish(2 * i - 2)
-                finish(2 * i - 1)
-            if i == sent_at:
-                scan_send(k, 0, 0)
-            for at, hook in hooks:
-                if i == at:
-                    hook()
-            if i == sent_at + 2:
-                scan_take(k, 0, 0)
-                scan_send(k, 1, 0)
+        lax.fori_loop(0, mid_steps, step, 0)
+        out_step(mid_steps - 1)
+        for y in range(rows - 4, rows):
+            finish(y)
         scan_send(k, 0, 1)
         for s in range(hops):
-            if s > 0:
-                scan_take(k, s, 0)
-                scan_send(k, s + 1, 0)
+            scan_take(k, s, 0)
+            scan_send(k, s + 1, 0)
             scan_take(k, s, 1)
             scan_send(k, s + 1, 1)
 
@@ -306,6 +300,9 @@
     def _():
         st[pl.ds(rows + RIM, RIM)] = jnp.zeros((RIM,) + st.shape[1:], bf16)
 
+    st[pl.ds(rows + 2 * RIM, 2)] = jnp.zeros((2,) + st.shape[1:], bf16)
+    middle[...] = jnp.zeros(middle.shape, f32)
+    parts[...] = jnp.zeros(parts.shape, f32)
     expand(x, RIM, rows)
     for i in (1, 2, 3, 5):
         loads[i].wait()
@@ -448,8 +445,9 @@
             vmem(frame, f32),
             vmem((hidden, 9 * chans), bf16),
             vmem((hidden, 9 * hidden), bf16),
-            vmem((rows + 2 * RIM, 3 * chans, cols), bf16),
-            vmem((rows + 4, 3 * hidden, cols), bf16),
+            vmem((rows + 2 * RIM + 2, 3 * chans, cols), bf16),
+            vmem((rows + 6, 3 * hidden, cols), bf16),
+            vmem((hidden, 2 * cols), f32),
             vmem((rows + 2, 9 * chans, cols), f32),
             vmem(frame, f32),
             vmem(frame, f32),

time: 81 us -> 75.6 us (0.933)
  the two profiles are of different devices: /device:TPU:25 before, /device:TPU:30 now
where the time goes in v3:
time: 75.6 us; the launch traced here: 75.4 us
  Pallas kernels  70 us (93%)
  local copies, waits for them, and re-layouts  3.94 us (5%)
  other arithmetic  1.22 us (2%)
    pallas_call x1, Pallas kernels, shards(): pl.pallas_call(functools.partial(kernel, n, strips, hops), out_shape=jax....  70 us
    broadcast_in_dim x1, local copies, waits for them, and re-layouts, shards(): return result.transpose(0, 2, 1, 3)[:, None, None]  1.73 us

profile of v3, /device:TPU:30, one launch (start us, length us, event | category | flops | bytes accessed | tf_op | source)
XLA Modules:
  0.0 75.4 jit_solution(18164148772181783919)
XLA Ops:
  0.0 0.0 copy-start
  0.0 0.0 copy-start.2
  0.0 0.7 copy-done.2
  0.7 0.1 dynamic-slice_bitcast_fusion.1
  0.8 0.0 copy-start.1
  0.8 0.1 convert_reduce_fusion
  0.9 0.1 eq.16
  1.0 0.5 copy-done.1
  1.5 0.2 select_reduce_fusion
  1.6 0.1 reshape.18
  1.7 0.1 multiply_sine_fusion
  1.9 0.0 copy-done
  1.9 0.2 fusion
  2.0 0.1 rsqrt_add_fusion
  2.2 0.7 pad_maximum_fusion.coef
  2.8 0.8 %broadcast_in_dim.27.emb = f32[2,192,128]{2,1,0:T(8,128)} broadcast(f32[2,192]{1,0:T(2,128)S(1)} %fusion), dimensions={0,1} | broadcast | bytes 198144 | tf_op jit(solution)/shard_map/broadcast_in_dim | solution.py:427
  3.6 70.0 %shard_map.91 = f32[2,16,16,128]{3,2,1,0:T(8,128)} custom-call(f32[2,3]{1,0:T(2,128)} %pad_maximum_fusion.coef, f32[1,16,16,128]{3,2,1,0:T(8,128)} %x_far.1, f32[1,1,16,16,128]{4,3,2,1,0:T(8,128)} %z_far.1, f32[5,1,16,16,128]{4,3,2,1,0:T(8,128)} %fresh_far.1, f32[2,192,128]{2,1,0:T(8,128)} %broadcast_in_dim.27.emb, bf16[144,192]{1,0:T(8,128)(2,1)} %bitcast.13, ...), custom_call_target="tpu_custom_call" | custom-call | flops 6341787648 | bytes 4194304 | tf_op jit(solution)/shard_map/pallas_call | solution.py:430
  73.6 1.7 %copy.12 = f32[2,1,1,16,16,128]{5,4,3,2,1,0:T(8,128)} copy(f32[2,1,1,16,16,128]{5,3,4,0,2,1:T(8,128)} %bitcast.12) | data formatting | bytes 524288 | tf_op jit(solution)/shard_map/broadcast_in_dim | solution.py:488
  (2 shorter events, 0.0 us)
Async XLA Ops:
  0.0 1.9 %copy-start = (bf16[192,192]{1,0:T(8,128)(2,1)S(1)}, bf16[192,192]{1,0:T(8,128)(2,1)}, u32[]{:S(2)}) copy-start(bf16[192,192]{1,0:T(8,128)(2,1)} %param.16) | copy-start | bytes 221188
  0.0 0.7 copy-start.2
  0.8 0.7 copy-start.1

commit v4 on v3

--- a/solution.py
+++ b/solution.py
@@ -53,13 +53,13 @@
 
 def moved_right(v):
     lane = lax.broadcasted_iota(jnp.int32, v.shape, v.ndim - 1)
-    return jnp.where(lane == 0, 0.0, pltpu.roll(v, 1, v.ndim - 1))
+    return jnp.where(lane == 0, jnp.zeros_like(v), pltpu.roll(v, 1, v.ndim - 1))
 
 
 def moved_left(v):
     size = v.shape[-1]
     lane = lax.broadcasted_iota(jnp.int32, v.shape, v.ndim - 1)
-    return jnp.where(lane == size - 1, 0.0, pltpu.roll(v, size - 1, v.ndim - 1))
+    return jnp.where(lane == size - 1, jnp.zeros_like(v), pltpu.roll(v, size - 1, v.ndim - 1))
 
 
 def kernel(
@@ -173,8 +173,8 @@
         return remote(nsnd.at[k, s], nrcv.at[k, s], nscan_ss.at[k, s], nscan_rs.at[k, s], to, strip)
 
     def spread_rows(v):
-        v = v.astype(f32)
-        return jnp.concatenate([moved_right(v), v, moved_left(v)], axis=-2).astype(bf16)
+        v = v.astype(bf16)
+        return jnp.concatenate([moved_right(v), v, moved_left(v)], axis=-2)
 
     def expand(source, at, count):
         for i in range(count):
@@ -258,13 +258,16 @@
         in_step(0, up_scale)
         in_step(1)
         lax.fori_loop(0, mid_steps, step, 0)
+        scan_take(k, 0, 0)
+        scan_send(k, 1, 0)
         out_step(mid_steps - 1)
         for y in range(rows - 4, rows):
             finish(y)
         scan_send(k, 0, 1)
         for s in range(hops):
-            scan_take(k, s, 0)
-            scan_send(k, s + 1, 0)
+            if s > 0:
+                scan_take(k, s, 0)
+                scan_send(k, s + 1, 0)
             scan_take(k, s, 1)
             scan_send(k, s + 1, 1)
 

time: 75.6 us -> 78.3 us (1.036)
  the two profiles are of different devices: /device:TPU:30 before, /device:TPU:25 now
where the time goes in v4:
time: 78.3 us; the launch traced here: 78 us
  Pallas kernels  72.6 us (93%)
  local copies, waits for them, and re-layouts  3.94 us (5%)
  other arithmetic  1.22 us (2%)
    pallas_call x1, Pallas kernels, shards(): pl.pallas_call(functools.partial(kernel, n, strips, hops), out_shape=jax....  72.6 us
    broadcast_in_dim x1, local copies, waits for them, and re-layouts, shards(): return result.transpose(0, 2, 1, 3)[:, None, None]  1.73 us

profile of v4, /device:TPU:25, one launch (start us, length us, event | category | flops | bytes accessed | tf_op | source)
XLA Modules:
  0.0 78.0 jit_solution(9863179086620975789)
XLA Ops:
  0.0 0.0 copy-start
  0.0 0.0 copy-start.2
  0.0 0.7 copy-done.2
  0.7 0.1 dynamic-slice_bitcast_fusion.1
  0.8 0.0 copy-start.1
  0.8 0.1 convert_reduce_fusion
  0.9 0.1 eq.16
  1.0 0.5 copy-done.1
  1.5 0.2 select_reduce_fusion
  1.6 0.1 reshape.18
  1.7 0.1 multiply_sine_fusion
  1.9 0.0 copy-done
  1.9 0.2 fusion
  2.0 0.1 rsqrt_add_fusion
  2.2 0.7 pad_maximum_fusion.coef
  2.8 0.8 %broadcast_in_dim.27.emb = f32[2,192,128]{2,1,0:T(8,128)} broadcast(f32[2,192]{1,0:T(2,128)S(1)} %fusion), dimensions={0,1} | broadcast | bytes 198144 | tf_op jit(solution)/shard_map/broadcast_in_dim | solution.py:430
  3.6 72.6 %shard_map.91 = f32[2,16,16,128]{3,2,1,0:T(8,128)} custom-call(f32[2,3]{1,0:T(2,128)} %pad_maximum_fusion.coef, f32[1,16,16,128]{3,2,1,0:T(8,128)} %x_far.1, f32[1,1,16,16,128]{4,3,2,1,0:T(8,128)} %z_far.1, f32[5,1,16,16,128]{4,3,2,1,0:T(8,128)} %fresh_far.1, f32[2,192,128]{2,1,0:T(8,128)} %broadcast_in_dim.27.emb, bf16[144,192]{1,0:T(8,128)(2,1)} %bitcast.13, ...), custom_call_target="tpu_custom_call" | custom-call | flops 6341787648 | bytes 4194304 | tf_op jit(solution)/shard_map/pallas_call | solution.py:433
  76.3 1.7 %copy.12 = f32[2,1,1,16,16,128]{5,4,3,2,1,0:T(8,128)} copy(f32[2,1,1,16,16,128]{5,3,4,0,2,1:T(8,128)} %bitcast.12) | data formatting | bytes 524288 | tf_op jit(solution)/shard_map/broadcast_in_dim | solution.py:491
  (2 shorter events, 0.0 us)
Async XLA Ops:
  0.0 1.9 %copy-start = (bf16[192,192]{1,0:T(8,128)(2,1)S(1)}, bf16[192,192]{1,0:T(8,128)(2,1)}, u32[]{:S(2)}) copy-start(bf16[192,192]{1,0:T(8,128)(2,1)} %param.16) | copy-start | bytes 221188
  0.0 0.7 copy-start.2
  0.8 0.7 copy-start.1

commit v5 on v3

--- a/solution.py
+++ b/solution.py
@@ -258,13 +258,16 @@
         in_step(0, up_scale)
         in_step(1)
         lax.fori_loop(0, mid_steps, step, 0)
+        scan_take(k, 0, 0)
+        scan_send(k, 1, 0)
         out_step(mid_steps - 1)
         for y in range(rows - 4, rows):
             finish(y)
         scan_send(k, 0, 1)
         for s in range(hops):
-            scan_take(k, s, 0)
-            scan_send(k, s + 1, 0)
+            if s > 0:
+                scan_take(k, s, 0)
+                scan_send(k, s + 1, 0)
             scan_take(k, s, 1)
             scan_send(k, s + 1, 1)
 

time: 75.6 us -> 78.3 us (1.036)
  the two profiles are of different devices: /device:TPU:30 before, /device:TPU:25 now
where the time goes in v5:
time: 78.3 us; the launch traced here: 78.1 us
  Pallas kernels  72.7 us (93%)
  local copies, waits for them, and re-layouts  3.94 us (5%)
  other arithmetic  1.22 us (2%)
    pallas_call x1, Pallas kernels, shards(): pl.pallas_call(functools.partial(kernel, n, strips, hops), out_shape=jax....  72.7 us
    broadcast_in_dim x1, local copies, waits for them, and re-layouts, shards(): return result.transpose(0, 2, 1, 3)[:, None, None]  1.73 us

profile of v5, /device:TPU:25, one launch (start us, length us, event | category | flops | bytes accessed | tf_op | source)
XLA Modules:
  0.0 78.1 jit_solution(13463480682283552731)
XLA Ops:
  0.0 0.0 copy-start
  0.0 0.0 copy-start.2
  0.0 0.7 copy-done.2
  0.7 0.1 dynamic-slice_bitcast_fusion.1
  0.8 0.0 copy-start.1
  0.8 0.1 convert_reduce_fusion
  0.9 0.1 eq.16
  1.0 0.5 copy-done.1
  1.5 0.2 select_reduce_fusion
  1.6 0.1 reshape.18
  1.7 0.1 multiply_sine_fusion
  1.9 0.0 copy-done
  1.9 0.2 fusion
  2.0 0.1 rsqrt_add_fusion
  2.2 0.7 pad_maximum_fusion.coef
  2.8 0.8 %broadcast_in_dim.27.emb = f32[2,192,128]{2,1,0:T(8,128)} broadcast(f32[2,192]{1,0:T(2,128)S(1)} %fusion), dimensions={0,1} | broadcast | bytes 198144 | tf_op jit(solution)/shard_map/broadcast_in_dim | solution.py:430
  3.6 72.7 %shard_map.91 = f32[2,16,16,128]{3,2,1,0:T(8,128)} custom-call(f32[2,3]{1,0:T(2,128)} %pad_maximum_fusion.coef, f32[1,16,16,128]{3,2,1,0:T(8,128)} %x_far.1, f32[1,1,16,16,128]{4,3,2,1,0:T(8,128)} %z_far.1, f32[5,1,16,16,128]{4,3,2,1,0:T(8,128)} %fresh_far.1, f32[2,192,128]{2,1,0:T(8,128)} %broadcast_in_dim.27.emb, bf16[144,192]{1,0:T(8,128)(2,1)} %bitcast.13, ...), custom_call_target="tpu_custom_call" | custom-call | flops 6341787648 | bytes 4194304 | tf_op jit(solution)/shard_map/pallas_call | solution.py:433
  76.3 1.7 %copy.12 = f32[2,1,1,16,16,128]{5,4,3,2,1,0:T(8,128)} copy(f32[2,1,1,16,16,128]{5,3,4,0,2,1:T(8,128)} %bitcast.12) | data formatting | bytes 524288 | tf_op jit(solution)/shard_map/broadcast_in_dim | solution.py:491
  (2 shorter events, 0.0 us)
Async XLA Ops:
  0.0 1.9 %copy-start = (bf16[192,192]{1,0:T(8,128)(2,1)S(1)}, bf16[192,192]{1,0:T(8,128)(2,1)}, u32[]{:S(2)}) copy-start(bf16[192,192]{1,0:T(8,128)(2,1)} %param.16) | copy-start | bytes 221188
  0.0 0.7 copy-start.2
  0.8 0.7 copy-start.1
